TPU v7x, 256 devices: a whole 4x4x8 slice. The times are simulated.
256 devices in a mesh: hst: 32 (over z_lo, x, core), kv: 8 (over z_hi, y).
Axes of the slice: x: 4, y: 4, z: 8 (z_hi: 2, z_lo: 4; z = z_hi * 4 + z_lo), core: 2. Of those that a mesh axis runs over, the one named last changes fastest.
Arguments:
- queries: bfloat16 [16384, 4096], P('hst', 'kv'), may hold values from -160 to 160
- keys: bfloat16 [16384, 1024], P('hst', 'kv'), may hold values from -4 to 4
- values: bfloat16 [16384, 1024], P('hst', 'kv'), may hold values from -4 to 4
- out_weight: bfloat16 [4096, 4096], P('kv'), may hold values from -0.09375 to 0.09375
- keep: int32 [32, 8, 256], P('hst', 'kv'), may hold values from 0 to 511, as said below
- anchor_len: int32 [8], P('kv'), may hold values from 64 to 256, as said below
Outputs:
- projected: bfloat16 [16384, 4096], P(('hst', 'kv'))
Inputs may be any that keep to these rules, and one draw needn't show every extreme that they name: `keep`: within one block and KV head the 256 positions are distinct. `anchor_len`: at least one KV head has 256 live anchor rows.
All inputs are finite; a program needn't handle non-finite values.
Results may differ from a plain program's by a relative error of at most 0.018.
Values may be sent and summed in bfloat16 or wider, within the bound.
A program may use at most 64 MiB of HBM per device.

v0:
```python
import math

import jax
import jax.numpy as jnp
from jax import lax
from jax.sharding import PartitionSpec as P

ANC = 256


NEGATIVE = -1e30


def from_root(block, axis, owner):
    block = jnp.where(lax.axis_index(axis) == owner, block, jnp.zeros_like(block))
    return lax.psum(block, axis)


def update(softmax_state, query_rows, key_rows, value_rows, allowed):
    running_max, running_sum, running_out = softmax_state
    scores = jnp.einsum("qhd,kd->hqk", query_rows, key_rows, preferred_element_type=jnp.float32)
    scores = scores * (1.0 / math.sqrt(key_rows.shape[1]))
    scores = jnp.where(allowed[None], scores, NEGATIVE)
    new_max = jnp.maximum(running_max, jnp.max(scores, -1))
    rescale = jnp.exp(running_max - new_max)
    weights = jnp.where(allowed[None], jnp.exp(scores - new_max[..., None]), 0.0)
    running_sum = running_sum * rescale + jnp.sum(weights, -1)
    products = jnp.einsum(
        "hqk,kd->hqd", weights.astype(jnp.bfloat16), value_rows, preferred_element_type=jnp.float32
    )
    running_out = running_out * rescale[..., None] + products
    return (new_max, running_sum, running_out)


def absorb_rows(softmax_state, query_rows, key_rows, value_rows, first_row, row_limit):
    total_rows = key_rows.shape[0]
    block_rows = query_rows.shape[0]
    slab_rows = total_rows
    while slab_rows > 512 and slab_rows % 2 == 0:
        slab_rows = slab_rows // 2
    rounds = total_rows // slab_rows

    def one_slab(round_index, folded):
        slab_keys = lax.dynamic_slice_in_dim(key_rows, round_index * slab_rows, slab_rows, 0)
        slab_values = lax.dynamic_slice_in_dim(value_rows, round_index * slab_rows, slab_rows, 0)
        row_ids = first_row + round_index * slab_rows + jnp.arange(slab_rows)
        allowed = jnp.broadcast_to((row_ids < row_limit)[None, :], (block_rows, slab_rows))
        return update(folded, query_rows, slab_keys, slab_values, allowed)

    return lax.fori_loop(0, rounds, one_slab, softmax_state)


def on_device(queries, keys, values, out_weight, keep, anchor_len):
    block_rows, head_width = keys.shape
    group_heads = queries.shape[1] // head_width
    keep_rows = keep.shape[2]
    query_rows = queries.reshape(block_rows, group_heads, head_width)
    host_index = lax.axis_index("hst")
    positions = jnp.arange(block_rows)
    onehot = (keep[0, 0][:, None] == positions[None, :]).astype(jnp.bfloat16)
    pass_keys = jnp.dot(onehot, keys, preferred_element_type=jnp.float32).astype(jnp.bfloat16)
    pass_values = jnp.dot(onehot, values, preferred_element_type=jnp.float32).astype(jnp.bfloat16)
    anchor_keys, anchor_values = (
        from_root(keys[:ANC], "hst", 0),
        from_root(values[:ANC], "hst", 0),
    )
    row_limit = host_index * keep_rows
    local_mask = positions[:, None] >= positions[None, :]
    anchor_ok = (jnp.arange(ANC) < anchor_len[0]) & (host_index > 0)
    anchor_mask = jnp.broadcast_to(anchor_ok[None, :], (block_rows, ANC))
    softmax_state = (
        jnp.full((group_heads, block_rows), NEGATIVE, jnp.float32),
        jnp.zeros((group_heads, block_rows), jnp.float32),
        jnp.zeros((group_heads, block_rows, head_width), jnp.float32),
    )
    softmax_state = update(softmax_state, query_rows, anchor_keys, anchor_values, anchor_mask)
    gathered_keys = lax.all_gather(pass_keys, "hst", axis=0, tiled=True)
    gathered_values = lax.all_gather(pass_values, "hst", axis=0, tiled=True)
    softmax_state = absorb_rows(
        softmax_state, query_rows, gathered_keys, gathered_values, 0, row_limit
    )
    softmax_state = update(softmax_state, query_rows, keys, values, local_mask)
    running_max, running_sum, running_out = softmax_state
    attended = (running_out / running_sum[..., None]).astype(jnp.bfloat16)
    attended = attended.transpose(1, 0, 2).reshape(block_rows, group_heads * head_width)
    return lax.psum_scatter(
        jnp.dot(attended, out_weight, preferred_element_type=jnp.float32).astype(jnp.bfloat16),
        "kv",
        scatter_dimension=0,
        tiled=True,
    )


def solution(mesh):
    placed = (
        P("hst", "kv"),
        P("hst", "kv"),
        P("hst", "kv"),
        P("kv", None),
        P("hst", "kv", None),
        P("kv"),
    )
    return jax.shard_map(
        on_device, mesh=mesh, in_specs=placed, out_specs=P(("hst", "kv"), None), check_vma=False
    )
```

profile of v0, /device:TPU:96, one launch (start us, length us, event | category | flops | bytes accessed | tf_op | source)
XLA Modules:
  0.0 621.7 jit_solution(6628058749787552310)
XLA Ops:
  6.5 1.5 slice_select_fusion
  8.0 1.5 slice_select_fusion.1
  9.6 1.8 convolution_convert_fusion.2
  11.5 1.8 convolution_convert_fusion.1
  14.0 1.3 copy.13
  15.6 3.7 fusion.21
  19.3 226.7 %all-reduce.3.cloned.1.call-done = (bf16[256,128]{1,0:T(8,128)(2,1)}, bf16[256,128]{1,0:T(8,128)(2,1)}) async-done(((bf16[256,128]{1,0:T(8,128)(2,1)}, bf16[256,128]{1,0:T(8,128)(2,1)}), (bf16[256,128]{1,0:T(8,128)(2,1)}, bf16[256,128]{1,0:T(8,128)(2,1)})) %all-reduce.3.cloned.1.call-update) | async-done | bytes 131088 | tf_op jit(solution)/shard_map/psum | solution.py:16
  246.1 1.3 bitcast_reduce_fusion.1
  249.0 76.1 %all-gather.3.cloned.1.call-done = bf16[8192,128]{1,0:T(8,128)(2,1)} async-done(((bf16[256,128]{1,0:T(8,128)(2,1)}), bf16[8192,128]{1,0:T(8,128)(2,1)}) %all-gather.3.cloned.1.call-update) | async-done | bytes 2097168 | tf_op jit(solution)/shard_map/all_gather | solution.py:77
  325.1 61.1 %all-gather.5.cloned.1.call-done = bf16[8192,128]{1,0:T(8,128)(2,1)} async-done(((bf16[256,128]{1,0:T(8,128)(2,1)}), bf16[8192,128]{1,0:T(8,128)(2,1)}) %all-gather.5.cloned.1.call-update) | async-done | bytes 2097168 | tf_op jit(solution)/shard_map/all_gather | solution.py:78
  386.2 94.8 %while.17 = (s32[]{:T(128)}, f32[4,512]{1,0:T(4,128)S(1)}, f32[4,512]{1,0:T(4,128)S(1)}, f32[4,512,128]{2,1,0:T(8,128)S(1)}, s32[]{:T(128)}, /*index=5*/bf16[819...) while((s32[]{:T(128)}, f32[4,512]{1,0:T(4,128)S(1)}, ...), condition=%wide.region_7.8_spmd, body=%wide.region_4.7_spmd.sunk | while | flops 551031808 | bytes 15600307 | solution.py:50
  386.2 1.7 bitcast_reduce_fusion.3
  387.9 1.2 fusion.73
  389.1 3.0 fusion.74
  392.1 1.7 bitcast_reduce_fusion.3
  393.8 1.2 fusion.73
  395.0 3.0 fusion.74
  398.0 1.7 bitcast_reduce_fusion.3
  399.7 1.2 fusion.73
  400.9 3.0 fusion.74
  404.0 1.7 bitcast_reduce_fusion.3
  405.7 1.2 fusion.73
  406.8 3.0 fusion.74
  409.9 1.7 bitcast_reduce_fusion.3
  411.6 1.2 fusion.73
  412.8 3.0 fusion.74
  415.8 1.7 bitcast_reduce_fusion.3
  417.5 1.2 fusion.73
  418.7 3.0 fusion.74
  421.8 1.7 bitcast_reduce_fusion.3
  423.4 1.2 fusion.73
  424.6 3.0 fusion.74
  427.7 1.7 bitcast_reduce_fusion.3
  429.4 1.2 fusion.73
  430.6 3.0 fusion.74
  433.6 1.7 bitcast_reduce_fusion.3
  435.3 1.2 fusion.73
  436.5 3.0 fusion.74
  439.5 1.7 bitcast_reduce_fusion.3
  441.2 1.2 fusion.73
  442.4 3.0 fusion.74
  445.5 1.7 bitcast_reduce_fusion.3
  447.2 1.2 fusion.73
  448.3 3.0 fusion.74
  451.4 1.7 bitcast_reduce_fusion.3
  453.1 1.2 fusion.73
  454.3 3.0 fusion.74
  457.3 1.7 bitcast_reduce_fusion.3
  459.0 1.2 fusion.73
  460.2 3.0 fusion.74
  463.3 1.7 bitcast_reduce_fusion.3
  464.9 1.2 fusion.73
  466.1 3.0 fusion.74
  469.2 1.7 bitcast_reduce_fusion.3
  470.9 1.2 fusion.73
  472.1 3.0 fusion.74
  475.1 1.7 bitcast_reduce_fusion.3
  476.8 1.2 fusion.73
  478.0 3.0 fusion.74
  481.4 3.4 fusion.22
  484.8 1.2 divide_convert_fusion
  486.0 1.0 copy-done.1
  487.0 4.4 convolution_convert_fusion
  491.4 123.7 %reduce-scatter.2.cloned.1.call-done = bf16[64,4096]{1,0:T(8,128)(2,1)} async-done(((bf16[512,4096]{1,0:T(8,128)(2,1)}), bf16[64,4096]{1,0:T(8,128)(2,1)}) %reduce-scatter.2.cloned.1.call-update) | async-done | bytes 524304 | tf_op jit(solution)/shard_map/reduce_scatter | solution.py:86
  (89 shorter events, 3.1 us)
Async XLA Ops:
  6.5 239.5 %all-reduce.3.cloned.1.call-start = ((), (), s32[]{:S(2)}) async-start(), calls=%async_computation.4 | async-start | bytes 262144 | tf_op jit(solution)/shard_map/psum | solution.py:16
  9.5 315.6 %all-gather.3.cloned.1.call-start = ((), (), s32[]{:S(2)}) async-start(), calls=%async_computation.1 | async-start | bytes 2162688 | tf_op jit(solution)/shard_map/all_gather | solution.py:77
  11.4 374.8 %all-gather.5.cloned.1.call-start = ((), (), s32[]{:S(2)}) async-start(), calls=%async_computation.2 | async-start | bytes 2162688 | tf_op jit(solution)/shard_map/all_gather | solution.py:78
  13.3 601.9 %reduce-scatter.2.cloned.1.call-start = ((), (), s32[]{:S(2)}) async-start(), calls=%async_computation.3 | async-start | bytes 4718592 | tf_op jit(solution)/shard_map/reduce_scatter | solution.py:86
  246.1 2.0 copy-start.3
  481.0 3.8 copy-start.2
  481.4 3.5 copy-start
  484.8 2.2 copy-start.1
Sparse Core Ops, SparseCore 0:
  10.0 235.9 all-reduce.2
  248.1 76.9 all-gather.2
  327.1 59.0 all-gather.4
  491.5 123.5 reduce-scatter.1
where the time goes:
time: 627 us; the launch traced here: 622 us
  waiting for transfers between devices  488 us (78%)
  matrix products  89.8 us (14%)
  other arithmetic  26.2 us (4%)
  between operations  13.9 us (2%)
    psum x1, waiting for transfers between devices, from_root(): return lax.psum(block, axis)  227 us
    reduce_scatter x1, waiting for transfers between devices, on_device(): lax.psum_scatter(jnp.dot(attended, out_weight, preferred_element_type=jnp...  124 us
    all_gather x1, waiting for transfers between devices, on_device(): gathered_keys = lax.all_gather(pass_keys, 'hst', axis=0, tiled=True)  76.1 us
    all_gather x1, waiting for transfers between devices, on_device(): gathered_values = lax.all_gather(pass_values, 'hst', axis=0, tiled=True)  61.1 us
    dot_general x18, matrix products, update(): jnp.einsum('hqk,kd->hqd', weights.astype(jnp.bfloat16), value_rows, prefe...  50.3 us
    dot_general x18, matrix products, update(): jnp.einsum('qhd,kd->hqk', query_rows, key_rows, preferred_element_type=jn...  31.5 us
    reduce_sum x18, other arithmetic, update(): running_sum = running_sum * rescale + jnp.sum(weights, -1)  22.6 us
  transfers between devices with their start and end apart: 4, of which 4 were waited for; matrix products, arithmetic and copies ran while one was open for 2% of the time, Pallas kernels for 0%

commit v1 on v0

v1 whole, which is shorter than its diff:
```python
import functools
import math

import jax
import jax.numpy as jnp
from jax import lax
from jax.experimental import pallas as pl
from jax.experimental.pallas import tpu as pltpu
from jax.sharding import PartitionSpec as P

HD = 128
QPG = 4
BLK = 512
KEEP = 256
NX, NZ, NY = 4, 4, 4
PLANE = 2 * NX
NCH = 4
ROWS = BLK // NCH
QROWS = QPG * ROWS
COLS = 1024
SCALE = math.log2(math.e) / math.sqrt(HD)
NEG = -1e30
F32, BF16 = jnp.float32, jnp.bfloat16
MESH = pl.DeviceIdType.MESH


def kernel(
    q_ref, k_ref, v_ref, keep_ref, alen_ref, w_ref, out_ref,
    kvown, kvbuf, qs, m_s, l_s, acc_s, xbuf, wbuf, ysc, yown, ysend, zbuf, fbuf,
    kv_send, kv_recv, w_send, w_recv, wl_send, wl_recv, w_own,
    x_send, x_recv, z_send, z_recv, o_send, o_recv,
):
    h = lax.axis_index("hst")
    g = lax.axis_index("kv")
    z, x, c = h // PLANE, (h % PLANE) // 2, h % 2
    zh, y = g // NY, g % NY
    right = z * PLANE + 2 * ((x + 1) % NX) + c
    left = z * PLANE + 2 * ((x + NX - 1) % NX) + c
    sib = z * PLANE + 2 * x + (1 - c)
    other = (1 - zh) * NY + y

    def at_y(d):
        return zh * NY + (y + d) % NY

    def remote(src, dst, send, recv, device):
        return pltpu.make_async_remote_copy(
            src_ref=src, dst_ref=dst, send_sem=send, recv_sem=recv,
            device_id=device, device_id_type=MESH,
        )

    def start(copy):
        copy.start()

    def sent(copy):
        copy.wait_send()

    barrier = pltpu.get_barrier_semaphore()
    partners = [(right, g), (left, g), (sib, g), (h, other)]
    partners += [(h, at_y(d)) for d in (1, 2, 3)]
    for device in partners:
        pl.semaphore_signal(barrier, inc=1, device_id=device, device_id_type=MESH)

    @pl.when(z < NZ - 1)
    def _():
        pl.semaphore_signal(barrier, inc=1, device_id=(h + PLANE, g), device_id_type=MESH)

    @pl.when(z > 0)
    def _():
        pl.semaphore_signal(barrier, inc=1, device_id=(h - PLANE, g), device_id_type=MESH)

    kvown[:, :HD] = k_ref[...]
    kvown[:, HD:] = v_ref[...]
    positions = lax.broadcasted_iota(jnp.int32, (BLK, KEEP), 0)
    onehot = (positions == keep_ref[...]).astype(F32).astype(BF16)
    kvbuf[h + 1] = lax.dot_general(
        onehot, kvown[...], (((0,), (0,)), ((), ())), preferred_element_type=F32
    ).astype(BF16)

    @pl.when(h == 0)
    def _():
        kvbuf[0] = kvown[:KEEP, :]

    n_partners = len(partners) + jnp.where(z < NZ - 1, 1, 0) + jnp.where(z > 0, 1, 0)
    pl.semaphore_wait(barrier, n_partners)

    half = BLK // 2

    def w_out(d):
        dst = (y + d) % NY
        return remote(
            w_ref.at[pl.ds(c * half, half), pl.ds(dst * COLS, COLS)],
            wbuf.at[y, pl.ds(c * half, half), :],
            w_send.at[d - 1], w_recv.at[d - 1], (h, at_y(d)),
        )

    def w_in(d):
        src = (y + NY - d) % NY
        ref = wbuf.at[src, pl.ds(c * half, half), :]
        return remote(ref, ref, w_send.at[d - 1], w_recv.at[d - 1], (h, at_y(NY - d)))

    def w_pass(d, core):
        src = (y + NY - d) % NY
        ref = wbuf.at[src, pl.ds(core * half, half), :]
        return remote(ref, ref, wl_send.at[d - 1], wl_recv.at[d - 1], (sib, g))

    w_local = pltpu.make_async_copy(w_ref.at[:, pl.ds(y * COLS, COLS)], wbuf.at[y], w_own)

    def kv_move(slot, device, kind, turn, act):
        ref = kvbuf.at[slot + 1]
        act(remote(ref, ref, kv_send.at[kind, turn], kv_recv.at[slot + 1], (device, g)))

        @pl.when(slot == 0)
        def _():
            anchor = kvbuf.at[0]
            act(remote(anchor, anchor, kv_send.at[kind, NZ], kv_recv.at[0], (device, g)))

    def kv_wait(slot):
        kv_move(slot, sib, 0, 0, lambda copy: copy.wait_recv())

    def column(turn, act):
        slot = (z - turn) * PLANE + 2 * x + c

        @pl.when(z < NZ - 1)
        def _():
            kv_move(slot, h + PLANE, 0, turn, act)

        kv_move(slot, right, 1, turn, act)
        kv_move(slot, left, 2, turn, act)
        kv_move(slot, sib, 3, turn, act)

    def side_slots(turn):
        base = (z - turn) * PLANE + c
        return base + 2 * ((x + NX - 1) % NX), base + 2 * ((x + 1) % NX)

    def sides(turn, act):
        from_left, from_right = side_slots(turn)
        kv_move(jnp.where(c == 0, from_left, from_right), jnp.where(c == 0, right, left), 4, turn, act)
        kv_move(from_left, sib, 5, turn, act)
        kv_move(from_right, sib, 6, turn, act)

    def opposite_slot(turn):
        return (z - turn) * PLANE + c + 2 * ((x + 2) % NX)

    def opposite(turn, act):
        kv_move(opposite_slot(turn), sib, 7, turn, act)

    def event_column(turn):
        @pl.when(turn > 0)
        def _():
            kv_wait((z - turn) * PLANE + 2 * x + c)

        column(turn, start)

    def event_sides(turn):
        for slot in side_slots(turn):
            kv_wait(slot)
        sides(turn, start)

    def event_opposite(turn):
        kv_wait(opposite_slot(turn))
        opposite(turn, start)

    def event_siblings(turn):
        for i in range(NX):
            kv_wait((z - turn) * PLANE + 2 * i + (1 - c))

    event_column(0)
    w_local.start()
    for d in (1, 2, 3):
        w_out(d).start()

    def prepare(j, carry):
        for i in range(QPG):
            rows = q_ref[:, pl.ds(j * 16, 16), i * HD : (i + 1) * HD]
            scaled = rows.reshape(ROWS, HD).astype(F32) * SCALE
            high = scaled.astype(BF16)
            qs[j, i * ROWS : (i + 1) * ROWS, :HD] = high
            qs[j, i * ROWS : (i + 1) * ROWS, HD:] = (scaled - high.astype(F32)).astype(BF16)
        m_s[j] = jnp.full((QROWS, HD), NEG, F32)
        l_s[j] = jnp.zeros((QROWS, HD), F32)
        acc_s[j] = jnp.zeros((QROWS, HD), F32)
        return carry

    lax.fori_loop(0, NCH, prepare, 0)

    def absorb(j, kv, bias):
        keys, vals = kv[:, :HD], kv[:, HD:]
        tiles = [slice(i * HD, (i + 1) * HD) for i in range(kv.shape[0] // HD)]
        scores = lax.dot_general(
            qs[j], jnp.concatenate([keys, keys], axis=1), (((1,), (1,)), ((), ())),
            preferred_element_type=F32,
        )
        scores = scores + bias
        top = functools.reduce(jnp.maximum, [scores[:, t] for t in tiles])
        old = m_s[j]
        new = jnp.maximum(old, jnp.max(top, axis=1, keepdims=True))
        rescale = jnp.exp2(old - new)
        weights = [jnp.exp2(scores[:, t] - new) for t in tiles]
        probs = jnp.concatenate([w.astype(BF16) for w in weights], axis=1)
        l_s[j] = l_s[j] * rescale + functools.reduce(jnp.add, weights)
        acc_s[j] = acc_s[j] * rescale + jnp.dot(probs, vals, preferred_element_type=F32)
        m_s[j] = new

    def column_bias(n, limit):
        return jnp.where(lax.broadcasted_iota(jnp.int32, (1, n), 1) < limit, 0.0, NEG).astype(F32)

    def absorb_plane(j, plane):
        n = PLANE * KEEP
        limit = jnp.where(plane == z, (h % PLANE) * KEEP, n)
        kv = kvbuf[pl.ds(plane * PLANE + 1, PLANE)].reshape(n, 2 * HD)
        absorb(j, kv, column_bias(n, limit))

    def local(j, carry):
        for at, event in ((1, event_sides), (2, event_opposite)):
            pl.when(j == at)(functools.partial(event, 0))
        row = lax.broadcasted_iota(jnp.int32, (QROWS, BLK), 0) % ROWS
        row = (row // 16) * 64 + j * 16 + row % 16
        key = lax.broadcasted_iota(jnp.int32, (QROWS, BLK), 1)
        absorb(j, kvown[...], jnp.where(key <= row, 0.0, NEG).astype(F32))
        return carry

    lax.fori_loop(0, NCH, local, 0)
    event_siblings(0)

    def turn_of(turn, carry):
        def quarter(j, inner):
            for at, event in ((0, event_column), (1, event_sides), (2, event_opposite)):
                pl.when(j == at)(functools.partial(event, turn))
            pl.when(z - turn + 1 >= 2)(lambda: absorb_plane(j, z - turn + 1))
            return inner

        lax.fori_loop(0, NCH, quarter, 0)
        event_siblings(turn)
        return carry

    lax.fori_loop(1, z + 1, turn_of, 0)

    w_local.wait()
    for d in (1, 2, 3):
        w_in(d).wait_recv()
        w_pass(d, c).start()

    def x_move(slot, j, to, kind, recv):
        ref = xbuf.at[slot, j]
        return remote(ref, ref, x_send.at[kind, j], x_recv.at[recv, j], (h, at_y(to)))

    def x_sends(j):
        return [x_move(y, j, 1, 0, 0), x_move(y, j, NY - 1, 1, 1)]

    def x_forward(j):
        slot = jnp.where(c == 0, (y + NY - 1) % NY, (y + 1) % NY)
        return x_move(slot, j, jnp.where(c == 0, 1, NY - 1), 2, 2)

    def x_wait(j, recv, d):
        x_move((y + d) % NY, j, 1, 0, recv).wait_recv()

    def z_move(j):
        return remote(ysend.at[j], zbuf.at[j], z_send.at[j], z_recv.at[j], (h, other))

    def o_move(j, d):
        to = (y + d) % NY
        return remote(
            fbuf.at[j, pl.ds(to * 16, 16), :],
            out_ref.at[pl.ds(j * 16, 16), pl.ds(y * COLS, COLS)],
            o_send.at[d - 1, j], o_recv.at[d - 1, j], (h, at_y(d)),
        )

    def o_wait(j, d):
        src = (y + NY - d) % NY
        ref = out_ref.at[pl.ds(j * 16, 16), pl.ds(src * COLS, COLS)]
        remote(ref, ref, o_send.at[d - 1, j], o_recv.at[d - 1, j], (h, at_y(d))).wait_recv()

    def attend(j):
        def one(i, carry):
            absorb_plane(j, jnp.minimum(z, 1) - i)
            return carry

        lax.fori_loop(0, jnp.minimum(z, 1) + 1, one, 0)
        absorb(j, kvbuf[0], column_bias(KEEP, jnp.where(h > 0, alen_ref[0], 0)))
        total = jnp.sum(l_s[j], axis=1, keepdims=True)
        attended = (acc_s[j] / total).astype(BF16)
        for i in range(QPG):
            xbuf[y, j, :, i * HD : (i + 1) * HD] = attended[i * ROWS : (i + 1) * ROWS]
        for copy in x_sends(j):
            copy.start()

    def relay(j):
        x_wait(j, 0, NY - 1)
        x_wait(j, 1, 1)
        x_forward(j).start()

    def project(j):
        @pl.when(j == 0)
        def _():
            for d in (1, 2, 3):
                w_pass(d, 1 - c).wait_recv()

        x_wait(j, 2, 2)
        ysc[...] = functools.reduce(
            jnp.add,
            [jnp.dot(xbuf[i, j], wbuf[i], preferred_element_type=F32) for i in range(NY)],
        )
        mine = ROWS // 2
        ysend[j] = ysc[pl.ds((1 - zh) * mine, mine), :].astype(BF16)
        z_move(j).start()
        yown[j] = ysc[pl.ds(zh * mine, mine), :]

    def finish(j):
        z_move(j).wait_recv()
        fbuf[j] = (yown[j] + zbuf[j].astype(F32)).astype(BF16)
        for d in (1, 2, 3):
            o_move(j, d).start()
        out_ref[pl.ds(j * 16, 16), pl.ds(y * COLS, COLS)] = fbuf[j, pl.ds(y * 16, 16), :]

    def tail(step, carry):
        for lag, stage in enumerate((attend, relay, project, finish)):
            j = step - lag
            pl.when((j >= 0) & (j < NCH))(functools.partial(stage, j))
        return carry

    lax.fori_loop(0, NCH + 3, tail, 0)

    for d in (1, 2, 3):
        w_out(d).wait_send()
        w_pass(d, c).wait_send()

    def drain(turn, carry):
        column(turn, sent)
        sides(turn, sent)
        opposite(turn, sent)
        return carry

    lax.fori_loop(0, z + 1, drain, 0)

    def drain_tail(j, carry):
        for copy in [*x_sends(j), x_forward(j), z_move(j)]:
            copy.wait_send()
        for d in (1, 2, 3):
            o_move(j, d).wait_send()
            o_wait(j, d)
        return carry

    lax.fori_loop(0, NCH, drain_tail, 0)


def on_device(queries, keys, values, out_weight, keep, anchor_len):
    vmem, dma = pltpu.VMEM, pltpu.SemaphoreType.DMA
    mine = ROWS // 2
    return pl.pallas_call(
        kernel,
        out_shape=jax.ShapeDtypeStruct((BLK // 8, 4 * COLS), BF16),
        in_specs=[pl.BlockSpec(memory_space=pltpu.VMEM)] * 4
        + [pl.BlockSpec(memory_space=pltpu.SMEM), pl.BlockSpec(memory_space=pl.ANY)],
        out_specs=pl.BlockSpec(memory_space=pltpu.VMEM),
        scratch_shapes=[
            vmem((BLK, 2 * HD), BF16),
            vmem((NZ * PLANE + 1, KEEP, 2 * HD), BF16),
            vmem((NCH, QROWS, 2 * HD), BF16),
            vmem((NCH, QROWS, HD), F32),
            vmem((NCH, QROWS, HD), F32),
            vmem((NCH, QROWS, HD), F32),
            vmem((NY, NCH, ROWS, QPG * HD), BF16),
            vmem((NY, BLK, COLS), BF16),
            vmem((ROWS, COLS), F32),
            vmem((NCH, mine, COLS), F32),
            vmem((NCH, mine, COLS), BF16),
            vmem((NCH, mine, COLS), BF16),
            vmem((NCH, mine, COLS), BF16),
            dma((8, NZ + 1)),
            dma((NZ * PLANE + 1,)),
            dma((3,)),
            dma((3,)),
            dma((3,)),
            dma((3,)),
            dma,
            dma((3, NCH)),
            dma((3, NCH)),
            dma((NCH,)),
            dma((NCH,)),
            dma((3, NCH)),
            dma((3, NCH)),
        ],
        compiler_params=pltpu.CompilerParams(
            collective_id=0, has_side_effects=True, vmem_limit_bytes=48 * 2**20
        ),
        cost_estimate=pl.CostEstimate(
            flops=11 * 10**9, bytes_accessed=7 * 10**6, transcendentals=18 * 10**6
        ),
    )(
        queries.reshape(8, BLK // 8, QPG * HD),
        keys,
        values,
        keep.reshape(1, KEEP),
        anchor_len,
        out_weight,
    )


def solution(mesh):
    placed = (
        P("hst", "kv"),
        P("hst", "kv"),
        P("hst", "kv"),
        P("kv", None),
        P("hst", "kv", None),
        P("kv"),
    )
    return jax.shard_map(
        on_device, mesh=mesh, in_specs=placed, out_specs=P(("hst", "kv"), None), check_vma=False
    )
```

time: 627 us -> 103 us (0.16)
  waiting for transfers between devices: 488 us -> 0 us
  Pallas kernels: 0 us -> 95.4 us
  matrix products: 89.8 us -> 0 us
  other arithmetic: 26.2 us -> 0 us
  between operations: 13.9 us -> 0.67 us
    psum x1 -> x0, waiting for transfers between devices: 227 us -> none  [from_root(): return lax.psum(block, axis)]
    all_gather x2 -> x0, waiting for transfers between devices: 137 us -> none  [the longest x1 76.1 us: on_device(): gathered_keys = lax.all_gather(pass_keys, 'hst', axis=0, tiled=True)]
    reduce_scatter x1 -> x0, waiting for transfers between devices: 124 us -> none  [on_device(): lax.psum_scatter(jnp.dot(attended, out_weight, preferred_element_type=jnp...]
    pallas_call x0 -> x1, Pallas kernels: none -> 95.4 us  [on_device(): pl.pallas_call(kernel, out_shape=jax.ShapeDtypeStruct((BLK // 8, 4 * COLS...]
    dot_general x39 -> x0, matrix products: 89.8 us -> none  [the longest x18 50.3 us: update(): jnp.einsum('hqk,kd->hqd', weights.astype(jnp.bfloat16), value_rows, prefe...]
    reduce_sum x18 -> x0, other arithmetic: 22.6 us -> none  [update(): running_sum = running_sum * rescale + jnp.sum(weights, -1)]
  transfers between devices with their start and end apart: 4 -> 0, of which waited for: 4 -> 0; matrix products, arithmetic and copies ran while one was open for 2% -> 0% of each run, Pallas kernels for 0% -> 0%
where the time goes in v1:
time: 103 us
  Pallas kernels  95.4 us (93%)
  local copies, waits for them, and re-layouts  6.5 us (6%)
    pallas_call x1, Pallas kernels, on_device(): pl.pallas_call(kernel, out_shape=jax.ShapeDtypeStruct((BLK // 8, 4 * COLS...  95.4 us
    unnamed x11, local copies, waits for them, and re-layouts  6.5 us

profile of v1, /device:TPU:96, one launch (start us, length us, event | category | flops | bytes accessed | tf_op | source)
XLA Modules:
  0.0 102.6 jit_solution(12988398341841855036)
XLA Ops:
  0.7 0.0 copy-start
  0.7 2.2 %copy-done = bf16[512,4096]{1,0:T(8,128)(2,1)S(1)} copy-done((bf16[512,4096]{1,0:T(8,128)(2,1)S(1)}, bf16[512,4096]{1,0:T(8,128)(2,1)}, u32[]{:S(2)}) %copy-start) | copy-done | bytes 4194328
  2.8 0.0 copy-start.1
  2.8 1.0 %copy-done.1 = bf16[512,512]{1,0:T(8,128)(2,1)S(1)} copy-done((bf16[512,512]{1,0:T(8,128)(2,1)S(1)}, bf16[512,512]{1,0:T(8,128)(2,1)}, u32[]{:S(2)}) %copy-start.1) | copy-done | bytes 524312
  3.9 0.0 copy-start.2
  3.9 0.9 copy-done.2
  4.8 0.0 copy-start.3
  4.8 0.9 copy-done.3
  5.7 0.0 copy-start.4
  5.7 0.7 copy-done.4
  6.4 95.4 %shard_map.64 = bf16[64,4096]{1,0:T(8,128)(2,1)S(1)} custom-call(bf16[8,64,512]{2,1,0:T(8,128)(2,1)S(1)} %bitcast.2, bf16[512,128]{1,0:T(8,128)(2,1)S(1)} %copy-done.2, bf16[512,128]{1,0:T(8,128)(2,1)S(1)} %copy-done.3, s32[1,256]{1,0:T(1,128)S(1)} %bitcast.3, s32[1]{0:T(128)S(6)} %copy.8.alen_ref, bf16[512,4096]{1,0:T(8,128)(2,1)S(1)} %copy-done), custom_call_target="tpu_custom_call" | custom-call | flops 11000000512 | bytes 7000000 | tf_op jit(solution)/shard_map/pallas_call | solution.py:349
  101.8 0.8 copy.9
Async XLA Ops:
  0.7 2.2 %copy-start = (bf16[512,4096]{1,0:T(8,128)(2,1)S(1)}, bf16[512,4096]{1,0:T(8,128)(2,1)}, u32[]{:S(2)}) copy-start(bf16[512,4096]{1,0:T(8,128)(2,1)} %w_ref.1) | copy-start | bytes 12582916
  2.8 1.0 %copy-start.1 = (bf16[512,512]{1,0:T(8,128)(2,1)S(1)}, bf16[512,512]{1,0:T(8,128)(2,1)}, u32[]{:S(2)}) copy-start(bf16[512,512]{1,0:T(8,128)(2,1)} %param.6) | copy-start | bytes 1572868
  3.9 0.9 copy-start.2
  4.8 0.9 copy-start.3
  5.7 0.7 copy-start.4

commit v2 on v1

v2 whole, which is shorter than its diff:
```python
import functools
import math

import jax
import jax.numpy as jnp
from jax import lax
from jax.experimental import pallas as pl
from jax.experimental.pallas import tpu as pltpu
from jax.sharding import PartitionSpec as P

HD = 128
QPG = 4
BLK = 512
KEEP = 256
NX, NZ, NY = 4, 4, 4
PLANE = 2 * NX
ANCHOR = NZ * PLANE
NCH = 4
ROWS = BLK // NCH
QROWS = QPG * ROWS
COLS = 1024
SCALE = math.log2(math.e) / math.sqrt(HD)
NEG = -1e30
F32, BF16 = jnp.float32, jnp.bfloat16
MESH = pl.DeviceIdType.MESH


def kernel(
    q_hbm, k_hbm, v_hbm, keep_hbm, alen_hbm, w_ref, out_ref,
    q_ref, keep_ref, alen_ref, in_sem,
    kvown, kvbuf, qs, m_s, l_s, acc_s, xbuf, wbuf, ysc, yown, ysend, zbuf, fbuf,
    kv_send, kv_recv, w_send, w_recv, wl_send, wl_recv, w_own,
    x_send, x_recv, z_send, z_recv, o_send, o_recv,
):
    h = lax.axis_index("hst")
    g = lax.axis_index("kv")
    z, x, c = h // PLANE, (h % PLANE) // 2, h % 2
    zh, y = g // NY, g % NY
    sib = z * PLANE + 2 * x + (1 - c)
    other = (1 - zh) * NY + y

    def at_x(d):
        return z * PLANE + 2 * ((x + d) % NX) + c

    def at_y(d):
        return zh * NY + (y + d) % NY

    def remote(src, dst, send, recv, device):
        return pltpu.make_async_remote_copy(
            src_ref=src, dst_ref=dst, send_sem=send, recv_sem=recv,
            device_id=device, device_id_type=MESH,
        )

    def start(copy):
        copy.start()

    def sent(copy):
        copy.wait_send()

    barrier = pltpu.get_barrier_semaphore()
    partners = [(sib, g), (h, other)]
    for d in (1, 2, 3):
        partners += [(at_x(d), g), (h, at_y(d)), ((h + d * PLANE) % (NZ * PLANE), g)]
    for device in partners:
        pl.semaphore_signal(barrier, inc=1, device_id=device, device_id_type=MESH)

    loads = [
        pltpu.make_async_copy(src, dst, in_sem.at[i])
        for i, (src, dst) in enumerate(
            [
                (k_hbm, kvown.at[:, pl.ds(0, HD)]),
                (v_hbm, kvown.at[:, pl.ds(HD, HD)]),
                (keep_hbm, keep_ref),
                (q_hbm, q_ref),
                (alen_hbm, alen_ref),
            ]
        )
    ]
    for copy in loads:
        copy.start()
    for copy in loads[:3]:
        copy.wait()

    def slot_of(xx, plane, core):
        return xx * 2 * NZ + plane * 2 + core

    positions = lax.broadcasted_iota(jnp.int32, (BLK, KEEP), 0)
    onehot = (positions == keep_ref[...]).astype(F32).astype(BF16)
    kvbuf[slot_of(x, z, c)] = lax.dot_general(
        onehot, kvown[...], (((0,), (0,)), ((), ())), preferred_element_type=F32
    ).astype(BF16)

    @pl.when(h == 0)
    def _():
        kvbuf[ANCHOR] = kvown[:KEEP, :]

    pl.semaphore_wait(barrier, len(partners))

    half = BLK // 2

    def w_out(d):
        dst = (y + d) % NY
        return remote(
            w_ref.at[pl.ds(c * half, half), pl.ds(dst * COLS, COLS)],
            wbuf.at[y, pl.ds(c * half, half), :],
            w_send.at[d - 1], w_recv.at[d - 1], (h, at_y(d)),
        )

    def w_in(d):
        src = (y + NY - d) % NY
        ref = wbuf.at[src, pl.ds(c * half, half), :]
        return remote(ref, ref, w_send.at[d - 1], w_recv.at[d - 1], (h, at_y(NY - d)))

    def w_pass(d, core):
        src = (y + NY - d) % NY
        ref = wbuf.at[src, pl.ds(core * half, half), :]
        return remote(ref, ref, wl_send.at[d - 1], wl_recv.at[d - 1], (sib, g))

    w_local = pltpu.make_async_copy(w_ref.at[:, pl.ds(y * COLS, COLS)], wbuf.at[y], w_own)

    def kv_move(slot, device, kind, turn, act):
        ref = kvbuf.at[slot]
        act(remote(ref, ref, kv_send.at[kind, turn], kv_recv.at[slot], (device, g)))

        @pl.when(slot == 0)
        def _():
            anchor = kvbuf.at[ANCHOR]
            at = NZ + turn if kind == 0 else NZ
            act(remote(anchor, anchor, kv_send.at[kind, at], kv_recv.at[ANCHOR], (device, g)))

    def kv_wait(xx, plane, core):
        kv_move(slot_of(xx, plane, core), sib, 0, 0, lambda copy: copy.wait_recv())

    def upward(act):
        for d in (1, 2, 3):

            @pl.when(z + d < NZ)
            def _():
                kv_move(slot_of(x, z, c), h + d * PLANE, 0, d - 1, act)

    def sideways(plane, act):
        slot = slot_of(x, plane, c)
        kv_move(slot, at_x(1), 1, plane, act)
        kv_move(slot, at_x(3), 2, plane, act)
        kv_move(slot, sib, 3, plane, act)
        kv_move(slot, at_x(2), 4, plane, act)

    def across(d, plane, act):
        kv_move(slot_of((x + d) % NX, plane, c), sib, 4 + d, plane, act)

    def each_plane(body):
        lax.fori_loop(0, z + 1, lambda plane, carry: (body(plane), carry)[1], 0)

    def event_column(turn):
        kv_wait(x, z - turn, c)
        sideways(z - turn, start)

    def event_side(d):
        def one(plane):
            kv_wait((x + d) % NX, plane, c)
            across(d, plane, start)

        each_plane(one)

    def event_sibling(d):
        each_plane(lambda plane: kv_wait((x + d) % NX, plane, 1 - c))

    upward(start)
    sideways(z, start)
    w_local.start()
    for d in (1, 2, 3):
        w_out(d).start()

    @pl.when(z % 2 == 0)
    def _():
        def clear(xx, carry):
            kvbuf[pl.ds(slot_of(xx, z + 1, 0), 2)] = jnp.zeros((2, KEEP, 2 * HD), BF16)
            return carry

        lax.fori_loop(0, NX, clear, 0)

    for copy in loads[3:]:
        copy.wait()

    def prepare(j, carry):
        for i in range(QPG):
            rows = q_ref[:, pl.ds(j * 16, 16), i * HD : (i + 1) * HD]
            scaled = rows.reshape(ROWS, HD).astype(F32) * SCALE
            high = scaled.astype(BF16)
            qs[j, i * ROWS : (i + 1) * ROWS, :HD] = high
            qs[j, i * ROWS : (i + 1) * ROWS, HD:] = (scaled - high.astype(F32)).astype(BF16)
        m_s[j] = jnp.full((QROWS, HD), NEG, F32)
        l_s[j] = jnp.zeros((QROWS, HD), F32)
        acc_s[j] = jnp.zeros((QROWS, HD), F32)
        return carry

    lax.fori_loop(0, NCH, prepare, 0)

    def absorb(j, kv, bias):
        keys, vals = kv[:, :HD], kv[:, HD:]
        tiles = [slice(i * HD, (i + 1) * HD) for i in range(kv.shape[0] // HD)]
        scores = lax.dot_general(
            qs[j], jnp.concatenate([keys, keys], axis=1), (((1,), (1,)), ((), ())),
            preferred_element_type=F32,
        )
        scores = scores + bias
        top = functools.reduce(jnp.maximum, [scores[:, t] for t in tiles])
        old = m_s[j]
        new = jnp.maximum(old, jnp.max(top, axis=1, keepdims=True))
        rescale = jnp.exp2(old - new)
        weights = [jnp.exp2(scores[:, t] - new) for t in tiles]
        probs = jnp.concatenate([w.astype(BF16) for w in weights], axis=1)
        l_s[j] = l_s[j] * rescale + functools.reduce(jnp.add, weights)
        acc_s[j] = acc_s[j] * rescale + jnp.dot(probs, vals, preferred_element_type=F32)
        m_s[j] = new

    def column_bias(n, limit):
        return jnp.where(lax.broadcasted_iota(jnp.int32, (1, n), 1) < limit, 0.0, NEG).astype(F32)

    def absorb_column(j, xx, first, planes):
        n = planes * 2 * KEEP
        own = jnp.where(xx < x, 2 * KEEP, jnp.where(xx == x, c * KEEP, 0))
        limit = z * 2 * KEEP + own - first * 2 * KEEP
        kv = kvbuf[pl.ds(slot_of(xx, first, 0), 2 * planes)].reshape(n, 2 * HD)
        absorb(j, kv, column_bias(n, limit))

    def each_chunk(body):
        lax.fori_loop(0, NCH, lambda j, carry: (body(j), carry)[1], 0, unroll=2)

    def local(j):
        row = lax.broadcasted_iota(jnp.int32, (QROWS, BLK), 0) % ROWS
        row = (row // 16) * 64 + j * 16 + row % 16
        key = lax.broadcasted_iota(jnp.int32, (QROWS, BLK), 1)
        absorb(j, kvown[...], jnp.where(key <= row, 0.0, NEG).astype(F32))

    each_chunk(local)

    pl.when(z >= 1)(functools.partial(event_column, 1))
    kv_wait(x, z, 1 - c)
    pl.when(z >= 1)(lambda: kv_wait(x, z - 1, 1 - c))
    each_chunk(lambda j: absorb_column(j, x, (z // 2) * 2, 2))
    for turn in (2, 3):
        pl.when(z >= turn)(functools.partial(event_column, turn))
    for turn in (2, 3):
        pl.when(z >= turn)(lambda: kv_wait(x, z - turn, 1 - c))
    pl.when(z >= 2)(lambda: each_chunk(lambda j: absorb_column(j, x, 0, 2)))

    event_side(3)
    event_side(1)

    def x_move(j, d):
        ref = xbuf.at[y, j]
        return remote(ref, ref, x_send.at[d - 1, j], x_recv.at[d - 1, j], (h, at_y(d)))

    def x_wait(j, d):
        ref = xbuf.at[(y + NY - d) % NY, j]
        remote(ref, ref, x_send.at[d - 1, j], x_recv.at[d - 1, j], (h, at_y(d))).wait_recv()

    def z_move(j):
        return remote(ysend.at[j], zbuf.at[j], z_send.at[j], z_recv.at[j], (h, other))

    def o_move(j, d):
        to = (y + d) % NY
        return remote(
            fbuf.at[j, pl.ds(to * 16, 16), :],
            out_ref.at[pl.ds(j * 16, 16), pl.ds(y * COLS, COLS)],
            o_send.at[d - 1, j], o_recv.at[d - 1, j], (h, at_y(d)),
        )

    def o_wait(j, d):
        src = (y + NY - d) % NY
        ref = out_ref.at[pl.ds(j * 16, 16), pl.ds(src * COLS, COLS)]
        remote(ref, ref, o_send.at[d - 1, j], o_recv.at[d - 1, j], (h, at_y(d))).wait_recv()

    def attend(j):
        def one(i, carry):
            d = jnp.where(i == 0, 3, i)

            @pl.when(j == 0)
            def _():
                pl.when(i == 2)(lambda: event_side(2))
                event_sibling(d)

            xx = (x + d) % NX
            pl.when(z >= 2)(lambda: absorb_column(j, xx, 0, 4))
            pl.when(z < 2)(lambda: absorb_column(j, xx, 0, 2))
            return carry

        lax.fori_loop(0, 3, one, 0)
        absorb(j, kvbuf[ANCHOR], column_bias(KEEP, jnp.where(h > 0, alen_ref[0], 0)))
        total = jnp.sum(l_s[j], axis=1, keepdims=True)
        attended = (acc_s[j] / total).astype(BF16)
        for i in range(QPG):
            xbuf[y, j, :, i * HD : (i + 1) * HD] = attended[i * ROWS : (i + 1) * ROWS]
        for d in (1, 3, 2):
            x_move(j, d).start()

        @pl.when(j == 1)
        def _():
            w_local.wait()
            for d in (1, 2, 3):
                w_in(d).wait_recv()
                w_pass(d, c).start()

    def project(j):
        @pl.when(j == 0)
        def _():
            for d in (1, 2, 3):
                w_pass(d, 1 - c).wait_recv()

        for d in (1, 2, 3):
            x_wait(j, d)
        ysc[...] = functools.reduce(
            jnp.add,
            [jnp.dot(xbuf[i, j], wbuf[i], preferred_element_type=F32) for i in range(NY)],
        )
        mine = ROWS // 2
        ysend[j] = ysc[pl.ds((1 - zh) * mine, mine), :].astype(BF16)
        z_move(j).start()
        yown[j] = ysc[pl.ds(zh * mine, mine), :]

    def finish(j):
        z_move(j).wait_recv()
        fbuf[j] = (yown[j] + zbuf[j].astype(F32)).astype(BF16)
        for d in (1, 2, 3):
            o_move(j, d).start()
        out_ref[pl.ds(j * 16, 16), pl.ds(y * COLS, COLS)] = fbuf[j, pl.ds(y * 16, 16), :]

    def tail(step, carry):
        for lag, stage in ((0, attend), (2, project), (3, finish)):
            j = step - lag
            pl.when((j >= 0) & (j < NCH))(functools.partial(stage, j))
        return carry

    lax.fori_loop(0, NCH + 3, tail, 0)

    for d in (1, 2, 3):
        w_out(d).wait_send()
        w_pass(d, c).wait_send()

    upward(sent)

    def drain(plane):
        sideways(plane, sent)
        for d in (1, 2, 3):
            across(d, plane, sent)

    each_plane(drain)

    def drain_tail(j, carry):
        z_move(j).wait_send()
        for d in (1, 2, 3):
            x_move(j, d).wait_send()
            o_move(j, d).wait_send()
            o_wait(j, d)
        return carry

    lax.fori_loop(0, NCH, drain_tail, 0)


def on_device(queries, keys, values, out_weight, keep, anchor_len):
    vmem, dma = pltpu.VMEM, pltpu.SemaphoreType.DMA
    mine = ROWS // 2
    return pl.pallas_call(
        kernel,
        out_shape=jax.ShapeDtypeStruct((BLK // 8, 4 * COLS), BF16),
        in_specs=[pl.BlockSpec(memory_space=pl.ANY)] * 6,
        out_specs=pl.BlockSpec(memory_space=pltpu.VMEM),
        scratch_shapes=[
            vmem((8, BLK // 8, QPG * HD), BF16),
            vmem((1, KEEP), jnp.int32),
            pltpu.SMEM((1,), jnp.int32),
            dma((5,)),
            vmem((BLK, 2 * HD), BF16),
            vmem((NZ * PLANE + 1, KEEP, 2 * HD), BF16),
            vmem((NCH, QROWS, 2 * HD), BF16),
            vmem((NCH, QROWS, HD), F32),
            vmem((NCH, QROWS, HD), F32),
            vmem((NCH, QROWS, HD), F32),
            vmem((NY, NCH, ROWS, QPG * HD), BF16),
            vmem((NY, BLK, COLS), BF16),
            vmem((ROWS, COLS), F32),
            vmem((NCH, mine, COLS), F32),
            vmem((NCH, mine, COLS), BF16),
            vmem((NCH, mine, COLS), BF16),
            vmem((NCH, mine, COLS), BF16),
            dma((8, NZ + 3)),
            dma((NZ * PLANE + 1,)),
            dma((3,)),
            dma((3,)),
            dma((3,)),
            dma((3,)),
            dma,
            dma((3, NCH)),
            dma((3, NCH)),
            dma((NCH,)),
            dma((NCH,)),
            dma((3, NCH)),
            dma((3, NCH)),
        ],
        compiler_params=pltpu.CompilerParams(
            collective_id=0, has_side_effects=True, vmem_limit_bytes=48 * 2**20
        ),
        cost_estimate=pl.CostEstimate(
            flops=11 * 10**9, bytes_accessed=7 * 10**6, transcendentals=18 * 10**6
        ),
    )(
        queries.reshape(8, BLK // 8, QPG * HD),
        keys,
        values,
        keep.reshape(1, KEEP),
        anchor_len,
        out_weight,
    )


def solution(mesh):
    placed = (
        P("hst", "kv"),
        P("hst", "kv"),
        P("hst", "kv"),
        P("kv", None),
        P("hst", "kv", None),
        P("kv"),
    )
    return jax.shard_map(
        on_device, mesh=mesh, in_specs=placed, out_specs=P(("hst", "kv"), None), check_vma=False
    )
```

time: 103 us -> 85.3 us (0.83)
  Pallas kernels: 95.4 us -> 77.8 us
    pallas_call x1, Pallas kernels: 95.4 us -> 77.8 us  [on_device(): pl.pallas_call(kernel, out_shape=jax.ShapeDtypeStruct((BLK // 8, 4 * COLS...]
where the time goes in v2:
time: 85.3 us; the launch traced here: 85 us
  Pallas kernels  77.8 us (91%)
  local copies, waits for them, and re-layouts  6.5 us (8%)
    pallas_call x1, Pallas kernels, on_device(): pl.pallas_call(kernel, out_shape=jax.ShapeDtypeStruct((BLK // 8, 4 * COLS...  77.8 us
    unnamed x11, local copies, waits for them, and re-layouts  6.5 us

profile of v2, /device:TPU:96, one launch (start us, length us, event | category | flops | bytes accessed | tf_op | source)
XLA Modules:
  0.0 85.0 jit_solution(14984073194061123946)
XLA Ops:
  0.7 0.0 copy-start
  0.7 2.2 %copy-done = bf16[512,4096]{1,0:T(8,128)(2,1)S(1)} copy-done((bf16[512,4096]{1,0:T(8,128)(2,1)S(1)}, bf16[512,4096]{1,0:T(8,128)(2,1)}, u32[]{:S(2)}) %copy-start) | copy-done | bytes 4194328
  2.8 0.0 copy-start.1
  2.8 1.0 %copy-done.1 = bf16[512,512]{1,0:T(8,128)(2,1)S(1)} copy-done((bf16[512,512]{1,0:T(8,128)(2,1)S(1)}, bf16[512,512]{1,0:T(8,128)(2,1)}, u32[]{:S(2)}) %copy-start.1) | copy-done | bytes 524312
  3.9 0.0 copy-start.2
  3.9 0.9 %copy-done.2 = bf16[512,128]{1,0:T(8,128)(2,1)S(1)} copy-done((bf16[512,128]{1,0:T(8,128)(2,1)S(1)}, bf16[512,128]{1,0:T(8,128)(2,1)}, u32[]{:S(2)}) %copy-start.2) | copy-done | bytes 131096
  4.8 0.0 copy-start.3
  4.8 0.9 %copy-done.3 = bf16[512,128]{1,0:T(8,128)(2,1)S(1)} copy-done((bf16[512,128]{1,0:T(8,128)(2,1)S(1)}, bf16[512,128]{1,0:T(8,128)(2,1)}, u32[]{:S(2)}) %copy-start.3) | copy-done | bytes 131096
  5.7 0.0 copy-start.4
  5.7 0.7 copy-done.4
  6.4 77.8 %shard_map.64 = bf16[64,4096]{1,0:T(8,128)(2,1)S(1)} custom-call(bf16[8,64,512]{2,1,0:T(8,128)(2,1)S(1)} %bitcast.2, bf16[512,128]{1,0:T(8,128)(2,1)S(1)} %copy-done.2, bf16[512,128]{1,0:T(8,128)(2,1)S(1)} %copy-done.3, s32[1,256]{1,0:T(1,128)S(1)} %bitcast.3, s32[1]{0:T(128)S(6)} %copy.8.alen_hbm, bf16[512,4096]{1,0:T(8,128)(2,1)S(1)} %copy-done), custom_call_target="tpu_custom_call" | custom-call | flops 11000000512 | bytes 7000000 | tf_op jit(solution)/shard_map/pallas_call | solution.py:364
  84.2 0.8 copy.9
Async XLA Ops:
  0.7 2.2 %copy-start = (bf16[512,4096]{1,0:T(8,128)(2,1)S(1)}, bf16[512,4096]{1,0:T(8,128)(2,1)}, u32[]{:S(2)}) copy-start(bf16[512,4096]{1,0:T(8,128)(2,1)} %w_ref.1) | copy-start | bytes 12582916
  2.8 1.0 %copy-start.1 = (bf16[512,512]{1,0:T(8,128)(2,1)S(1)}, bf16[512,512]{1,0:T(8,128)(2,1)}, u32[]{:S(2)}) copy-start(bf16[512,512]{1,0:T(8,128)(2,1)} %param.6) | copy-start | bytes 1572868
  3.9 0.9 %copy-start.2 = (bf16[512,128]{1,0:T(8,128)(2,1)S(1)}, bf16[512,128]{1,0:T(8,128)(2,1)}, u32[]{:S(2)}) copy-start(bf16[512,128]{1,0:T(8,128)(2,1)} %k_hbm.1) | copy-start | bytes 393220
  4.8 0.9 %copy-start.3 = (bf16[512,128]{1,0:T(8,128)(2,1)S(1)}, bf16[512,128]{1,0:T(8,128)(2,1)}, u32[]{:S(2)}) copy-start(bf16[512,128]{1,0:T(8,128)(2,1)} %v_hbm.1) | copy-start | bytes 393220
  5.7 0.7 copy-start.4

commit v3 on v2

--- a/solution.py
+++ b/solution.py
@@ -138,35 +138,39 @@
             def _():
                 kv_move(slot_of(x, z, c), h + d * PLANE, 0, d - 1, act)
 
-    def sideways(plane, act):
+    def sideways(turn, act):
+        plane = z - turn
         slot = slot_of(x, plane, c)
         kv_move(slot, at_x(1), 1, plane, act)
         kv_move(slot, at_x(3), 2, plane, act)
         kv_move(slot, sib, 3, plane, act)
         kv_move(slot, at_x(2), 4, plane, act)
 
-    def across(d, plane, act):
+    def across(d, turn, act):
+        plane = z - turn
         kv_move(slot_of((x + d) % NX, plane, c), sib, 4 + d, plane, act)
-
-    def each_plane(body):
-        lax.fori_loop(0, z + 1, lambda plane, carry: (body(plane), carry)[1], 0)
 
     def event_column(turn):
         kv_wait(x, z - turn, c)
-        sideways(z - turn, start)
-
-    def event_side(d):
-        def one(plane):
-            kv_wait((x + d) % NX, plane, c)
-            across(d, plane, start)
-
-        each_plane(one)
-
-    def event_sibling(d):
-        each_plane(lambda plane: kv_wait((x + d) % NX, plane, 1 - c))
+        sideways(turn, start)
+
+    def event_sides(turn):
+        for d in (3, 1):
+            kv_wait((x + d) % NX, z - turn, c)
+            across(d, turn, start)
+
+    def event_opposite(turn):
+        kv_wait((x + 2) % NX, z - turn, c)
+        across(2, turn, start)
+
+    def event_sibling(d, turn):
+        kv_wait((x + d) % NX, z - turn, 1 - c)
+
+    def event(what, turn, *args):
+        pl.when(z >= turn)(lambda: what(*args, turn))
 
     upward(start)
-    sideways(z, start)
+    sideways(0, start)
     w_local.start()
     for d in (1, 2, 3):
         w_out(d).start()
@@ -235,18 +239,25 @@
 
     each_chunk(local)
 
-    pl.when(z >= 1)(functools.partial(event_column, 1))
-    kv_wait(x, z, 1 - c)
-    pl.when(z >= 1)(lambda: kv_wait(x, z - 1, 1 - c))
-    each_chunk(lambda j: absorb_column(j, x, (z // 2) * 2, 2))
-    for turn in (2, 3):
-        pl.when(z >= turn)(functools.partial(event_column, turn))
-    for turn in (2, 3):
-        pl.when(z >= turn)(lambda: kv_wait(x, z - turn, 1 - c))
-    pl.when(z >= 2)(lambda: each_chunk(lambda j: absorb_column(j, x, 0, 2)))
-
-    event_side(3)
-    event_side(1)
+    def half_column(d):
+        event(event_sibling, 0, d)
+        event(event_sibling, 1, d)
+        each_chunk(lambda j: absorb_column(j, (x + d) % NX, z // 2 * 2, 2))
+
+    event(event_column, 1)
+    half_column(0)
+    event(event_column, 2)
+    event(event_column, 3)
+    event(event_sides, 0)
+    event(event_sides, 1)
+    pl.when(z >= 2)(lambda: half_column(3))
+    event(event_opposite, 0)
+    event(event_opposite, 1)
+    pl.when(z >= 2)(lambda: half_column(1))
+    pl.when(z >= 2)(lambda: half_column(2))
+    event(event_sides, 2)
+    event(event_opposite, 2)
+    event(event_sides, 3)
 
     def x_move(j, d):
         ref = xbuf.at[y, j]
@@ -274,19 +285,19 @@
 
     def attend(j):
         def one(i, carry):
-            d = jnp.where(i == 0, 3, i)
+            d = jnp.where(i == 0, 0, jnp.where(i == 1, 3, jnp.where(i == 2, 1, 2)))
 
             @pl.when(j == 0)
             def _():
-                pl.when(i == 2)(lambda: event_side(2))
-                event_sibling(d)
-
-            xx = (x + d) % NX
-            pl.when(z >= 2)(lambda: absorb_column(j, xx, 0, 4))
-            pl.when(z < 2)(lambda: absorb_column(j, xx, 0, 2))
+                pl.when((i == 3) & (z >= 3))(lambda: event_opposite(3))
+                turn = jnp.where(z >= 2, 2, 0)
+                event(event_sibling, turn, d)
+                event(event_sibling, turn + 1, d)
+
+            absorb_column(j, (x + d) % NX, 0, 2)
             return carry
 
-        lax.fori_loop(0, 3, one, 0)
+        lax.fori_loop(jnp.where(z >= 2, 0, 1), 4, one, 0)
         absorb(j, kvbuf[ANCHOR], column_bias(KEEP, jnp.where(h > 0, alen_ref[0], 0)))
         total = jnp.sum(l_s[j], axis=1, keepdims=True)
         attended = (acc_s[j] / total).astype(BF16)
@@ -340,12 +351,13 @@
 
     upward(sent)
 
-    def drain(plane):
-        sideways(plane, sent)
+    def drain(turn, carry):
+        sideways(turn, sent)
         for d in (1, 2, 3):
-            across(d, plane, sent)
-
-    each_plane(drain)
+            across(d, turn, sent)
+        return carry
+
+    lax.fori_loop(0, z + 1, drain, 0)
 
     def drain_tail(j, carry):
         z_move(j).wait_send()
@@ -399,7 +411,7 @@
             dma((3, NCH)),
         ],
         compiler_params=pltpu.CompilerParams(
-            collective_id=0, has_side_effects=True, vmem_limit_bytes=48 * 2**20
+            collective_id=0, has_side_effects=True, vmem_limit_bytes=60 * 2**20
         ),
         cost_estimate=pl.CostEstimate(
             flops=11 * 10**9, bytes_accessed=7 * 10**6, transcendentals=18 * 10**6

time: 85.3 us -> 81 us (0.950)
  local copies, waits for them, and re-layouts: 6.5 us -> 1.87 us
    unnamed x11 -> x1, local copies, waits for them, and re-layouts: 6.5 us -> 1.87 us
where the time goes in v3:
time: 81 us; the launch traced here: 80.8 us
  Pallas kernels  78.3 us (97%)
  local copies, waits for them, and re-layouts  1.87 us (2%)
    pallas_call x1, Pallas kernels, on_device(): pl.pallas_call(kernel, out_shape=jax.ShapeDtypeStruct((BLK // 8, 4 * COLS...  78.3 us
    unnamed x1, local copies, waits for them, and re-layouts  1.87 us

profile of v3, /device:TPU:96, one launch (start us, length us, event | category | flops | bytes accessed | tf_op | source)
XLA Modules:
  0.0 80.8 jit_solution(17596458358112173297)
XLA Ops:
  0.7 78.3 %shard_map.64 = bf16[64,4096]{1,0:T(8,128)(2,1)} custom-call(bf16[8,64,512]{2,1,0:T(8,128)(2,1)} %bitcast.2, bf16[512,128]{1,0:T(8,128)(2,1)} %k_hbm.1, bf16[512,128]{1,0:T(8,128)(2,1)} %v_hbm.1, s32[1,256]{1,0:T(1,128)} %bitcast.3, s32[1]{0:T(128)S(6)} %copy.8.alen_hbm, bf16[512,4096]{1,0:T(8,128)(2,1)} %w_ref.1), custom_call_target="tpu_custom_call" | custom-call | flops 11000000512 | bytes 7000000 | tf_op jit(solution)/shard_map/pallas_call | solution.py:376
  79.0 1.9 %copy.9 = bf16[64,4096]{1,0:T(8,128)(2,1)} copy(bf16[64,4096]{1,0:T(8,128)(2,1)} %shard_map.64) | data formatting | bytes 1048576

commit v4 on v3

--- a/solution.py
+++ b/solution.py
@@ -239,23 +239,33 @@
 
     each_chunk(local)
 
-    def half_column(d):
-        event(event_sibling, 0, d)
-        event(event_sibling, 1, d)
-        each_chunk(lambda j: absorb_column(j, (x + d) % NX, z // 2 * 2, 2))
-
-    event(event_column, 1)
-    half_column(0)
-    event(event_column, 2)
-    event(event_column, 3)
-    event(event_sides, 0)
-    event(event_sides, 1)
-    pl.when(z >= 2)(lambda: half_column(3))
-    event(event_opposite, 0)
-    event(event_opposite, 1)
-    pl.when(z >= 2)(lambda: half_column(1))
-    pl.when(z >= 2)(lambda: half_column(2))
-    event(event_sides, 2)
+    arrivals = {
+        0: ((event_column, 1),),
+        1: ((event_column, 2), (event_column, 3), (event_sides, 0), (event_sides, 1)),
+        2: ((event_opposite, 0), (event_opposite, 1)),
+        3: ((event_sides, 2),),
+    }
+
+    def half_column(i, carry):
+        for at, due in arrivals.items():
+
+            @pl.when(i == at)
+            def _():
+                for what, turn in due:
+                    event(what, turn)
+
+        d = jnp.where(i == 0, 0, jnp.where(i == 1, 3, i - 1))
+
+        @pl.when((z >= 2) | (i == 0))
+        def _():
+            event(event_sibling, 0, d)
+            event(event_sibling, 1, d)
+            first = z // 2 * 2
+            each_chunk(lambda j: absorb_column(j, (x + d) % NX, first, 2))
+
+        return carry
+
+    lax.fori_loop(0, 4, half_column, 0)
     event(event_opposite, 2)
     event(event_sides, 3)
 
@@ -285,7 +295,7 @@
 
     def attend(j):
         def one(i, carry):
-            d = jnp.where(i == 0, 0, jnp.where(i == 1, 3, jnp.where(i == 2, 1, 2)))
+            d = jnp.where(i == 0, 0, jnp.where(i == 1, 3, i - 1))
 
             @pl.when(j == 0)
             def _():

time: 81 us -> 80.7 us (level)
  no operation moved by 1% of the time
where the time goes in v4:
time: 80.7 us; the launch traced here: 80.5 us
  Pallas kernels  78 us (97%)
  local copies, waits for them, and re-layouts  1.87 us (2%)
    pallas_call x1, Pallas kernels, on_device(): pl.pallas_call(kernel, out_shape=jax.ShapeDtypeStruct((BLK // 8, 4 * COLS...  78 us
    unnamed x1, local copies, waits for them, and re-layouts  1.87 us

profile of v4, /device:TPU:96, one launch (start us, length us, event | category | flops | bytes accessed | tf_op | source)
XLA Modules:
  0.0 80.5 jit_solution(1624939076110436435)
XLA Ops:
  0.7 78.0 %shard_map.64 = bf16[64,4096]{1,0:T(8,128)(2,1)} custom-call(bf16[8,64,512]{2,1,0:T(8,128)(2,1)} %bitcast.2, bf16[512,128]{1,0:T(8,128)(2,1)} %k_hbm.1, bf16[512,128]{1,0:T(8,128)(2,1)} %v_hbm.1, s32[1,256]{1,0:T(1,128)} %bitcast.3, s32[1]{0:T(128)S(6)} %copy.8.alen_hbm, bf16[512,4096]{1,0:T(8,128)(2,1)} %w_ref.1), custom_call_target="tpu_custom_call" | custom-call | flops 11000000512 | bytes 7000000 | tf_op jit(solution)/shard_map/pallas_call | solution.py:386
  78.7 1.9 %copy.9 = bf16[64,4096]{1,0:T(8,128)(2,1)} copy(bf16[64,4096]{1,0:T(8,128)(2,1)} %shard_map.64) | data formatting | bytes 1048576

commit v5 on v4

--- a/solution.py
+++ b/solution.py
@@ -299,7 +299,7 @@
 
             @pl.when(j == 0)
             def _():
-                pl.when((i == 3) & (z >= 3))(lambda: event_opposite(3))
+                pl.when((i == 2) & (z >= 3))(lambda: event_opposite(3))
                 turn = jnp.where(z >= 2, 2, 0)
                 event(event_sibling, turn, d)
                 event(event_sibling, turn + 1, d)

time: 80.7 us -> 79.8 us (0.989)
    pallas_call x1, Pallas kernels: 78 us -> 77.2 us  [on_device(): pl.pallas_call(kernel, out_shape=jax.ShapeDtypeStruct((BLK // 8, 4 * COLS...]
where the time goes in v5:
time: 79.8 us; the launch traced here: 79.7 us
  Pallas kernels  77.2 us (97%)
  local copies, waits for them, and re-layouts  1.87 us (2%)
    pallas_call x1, Pallas kernels, on_device(): pl.pallas_call(kernel, out_shape=jax.ShapeDtypeStruct((BLK // 8, 4 * COLS...  77.2 us
    unnamed x1, local copies, waits for them, and re-layouts  1.87 us

profile of v5, /device:TPU:96, one launch (start us, length us, event | category | flops | bytes accessed | tf_op | source)
XLA Modules:
  0.0 79.7 jit_solution(1990396028845756436)
XLA Ops:
  0.7 77.2 %shard_map.64 = bf16[64,4096]{1,0:T(8,128)(2,1)} custom-call(bf16[8,64,512]{2,1,0:T(8,128)(2,1)} %bitcast.2, bf16[512,128]{1,0:T(8,128)(2,1)} %k_hbm.1, bf16[512,128]{1,0:T(8,128)(2,1)} %v_hbm.1, s32[1,256]{1,0:T(1,128)} %bitcast.3, s32[1]{0:T(128)S(6)} %copy.8.alen_hbm, bf16[512,4096]{1,0:T(8,128)(2,1)} %w_ref.1), custom_call_target="tpu_custom_call" | custom-call | flops 11000000512 | bytes 7000000 | tf_op jit(solution)/shard_map/pallas_call | solution.py:386
  77.8 1.9 %copy.9 = bf16[64,4096]{1,0:T(8,128)(2,1)} copy(bf16[64,4096]{1,0:T(8,128)(2,1)} %shard_map.64) | data formatting | bytes 1048576
